TPU v7x, 512 devices: a whole 4x4x16 slice. The times are simulated.
512 devices in a mesh: kvp: 64 (over z, y), tp: 8 (over x, core).
Axes of the slice: x: 4, y: 4, z: 16, core: 2. Of those that a mesh axis runs over, the one named last changes fastest.
Arguments:
- query: bfloat16 [4, 128, 128], P(None, 'tp'), may hold values from -1000 to 1000
- key_cache: bfloat16 [4, 8, 16384, 128], P(None, 'tp', 'kvp'), may hold values from -4 to 4
- value_cache: bfloat16 [4, 8, 16384, 128], P(None, 'tp', 'kvp'), may hold values from -6 to 6
- lengths: int32 [4], replicated, may hold values from 2048 to 16384, as said below
- out_weight: bfloat16 [16384, 16384], P('tp', 'kvp'), may hold values from -0.046875 to 0.046875
- residual: bfloat16 [4, 16384], P(None, 'kvp'), may hold values from -0.3125 to 0.3125
- norm_gain: float32 [16384], P('kvp'), may hold values from 0.5 to 1.5
- gate_weight: bfloat16 [16384, 26624], P('kvp', 'tp'), may hold values from -0.046875 to 0.046875
- up_weight: bfloat16 [16384, 26624], P('kvp', 'tp'), may hold values from -0.046875 to 0.046875
Outputs:
- stream: bfloat16 [4, 16384], P(None, 'kvp')
- hidden: bfloat16 [4, 26624], P(None, 'tp')
Inputs may be any that keep to these rules, and one draw needn't show every extreme that they name: `lengths`: at least one sequence has exactly 16384 live positions and one has exactly 2048.
All inputs are finite; a program needn't handle non-finite values.
Results may differ from a plain program's by a relative error of at most 0.028.
Values may be sent and summed in bfloat16 or wider, within the bound.
No kernel may reach another device: no remote copies, remote signals or barrier semaphores. Data moves between devices by JAX's collectives and lax.ppermute only.
A program may use at most 64 MiB of HBM per device.

v0:
```python
import jax
import jax.numpy as jnp
from jax import lax
from jax.sharding import PartitionSpec as P


def combined_all(value, axis, join):
    pieces = jax.tree.map(lambda part: lax.all_gather(part, axis), value)
    head = jax.tree.map(lambda part: part[0], pieces)
    tail = jax.tree.map(lambda part: part[1:], pieces)
    running, _ = lax.scan(lambda running, section: (join(running, section), None), head, tail)
    return running


def join_parts(left_part, right_part):
    left_out, left_peak, left_sum = left_part
    right_out, right_peak, right_sum = right_part
    peak_both = jnp.maximum(left_peak, right_peak)
    left_factor = jnp.exp(left_peak - peak_both)
    right_factor = jnp.exp(right_peak - peak_both)
    joined = left_out * left_factor[..., None] + right_out * right_factor[..., None]
    return (joined, peak_both, left_sum * left_factor + right_sum * right_factor)


def local(
    query, key_cache, value_cache, lengths, out_weight, residual, norm_gain, gate_weight, up_weight
):
    row_count, heads_dev, head_dim = query.shape
    kv_dev = key_cache.shape[1]
    ctx_span = key_cache.shape[2]
    groups = heads_dev // kv_dev
    feat_width = heads_dev * head_dim
    queries = query.reshape(row_count, kv_dev, groups, head_dim)
    scores = jnp.einsum(
        "rkgd,rkpd->rkgp", queries, key_cache, preferred_element_type=jnp.float32
    ) * head_dim ** (-0.5)
    positions = lax.axis_index("kvp") * ctx_span + jnp.arange(ctx_span, dtype=jnp.int32)
    is_valid = (positions[None, :] < lengths[:, None])[:, None, None, :]
    masked = jnp.where(is_valid, scores, -1e30)
    top_score = jnp.max(masked, axis=-1)
    weights = jnp.where(is_valid, jnp.exp(masked - top_score[..., None]), 0.0)
    weight_sum = jnp.sum(weights, axis=-1)
    partial_value = jnp.einsum(
        "rkgp,rkpd->rkgd",
        weights.astype(jnp.bfloat16),
        value_cache,
        preferred_element_type=jnp.float32,
    )
    partial_value, top_score, weight_sum = combined_all(
        (partial_value, top_score, weight_sum), "kvp", join_parts
    )
    attention = (
        (partial_value / weight_sum[..., None]).reshape(row_count, feat_width).astype(jnp.bfloat16)
    )
    projected = jnp.dot(attention, out_weight, preferred_element_type=jnp.float32)
    mixed = residual.astype(jnp.float32) + lax.psum(projected, "tp")
    squares = lax.psum(jnp.sum(mixed * mixed, axis=1), "kvp")
    inv_rms = lax.rsqrt(squares / (mixed.shape[1] * lax.axis_size("kvp")) + 1e-05)
    normed = (mixed * inv_rms[:, None] * norm_gain).astype(jnp.bfloat16)
    gate_part = jnp.dot(normed, gate_weight, preferred_element_type=jnp.float32)
    up_part = jnp.dot(normed, up_weight, preferred_element_type=jnp.float32)
    gate_sum, up_sum = lax.psum((gate_part, up_part), "kvp")
    hidden = (jax.nn.silu(gate_sum) * up_sum).astype(jnp.bfloat16)
    return (mixed.astype(jnp.bfloat16), hidden)


def solution(mesh):
    placed = (
        P(None, "tp", None),
        P(None, "tp", "kvp", None),
        P(None, "tp", "kvp", None),
        P(),
        P("tp", "kvp"),
        P(None, "kvp"),
        P("kvp"),
        P("kvp", "tp"),
        P("kvp", "tp"),
    )
    return jax.shard_map(
        local,
        mesh=mesh,
        in_specs=placed,
        out_specs=(P(None, "kvp"), P(None, "tp")),
        check_vma=False,
    )
```

profile of v0, /device:TPU:2, one launch (start us, length us, event | category | flops | bytes accessed | tf_op | source)
XLA Modules:
  0.0 779.3 jit_solution(7362814043536033490)
XLA Ops:
  8.1 1.2 fusion.23
  9.3 1.8 fusion.6
  11.3 106.3 %all-gather.4 = f32[64,4,16]{2,1,0:T(4,128)S(1)} all-gather(f32[1,4,16]{2,1,0:T(4,128)S(1)} %bitcast.73), channel_id=4, replica_groups=mesh['kvp'=64,'tp'=8] {'kvp'}, dimensions={0}, use_global_device_ids=true | all-gather | bytes 16640 | tf_op jit(solution)/shard_map/all_gather | solution.py:8
  117.6 98.2 %all-gather.3 = f32[64,4,16]{2,1,0:T(4,128)S(1)} all-gather(f32[1,4,16]{2,1,0:T(4,128)S(1)} %bitcast.72), channel_id=3, replica_groups=mesh['kvp'=64,'tp'=8] {'kvp'}, dimensions={0}, use_global_device_ids=true | all-gather | bytes 16640 | tf_op jit(solution)/shard_map/all_gather | solution.py:8
  217.9 3.0 slice.38
  220.9 141.8 %while.14 = (s32[]{:T(128)}, f32[4,1,16,128]{3,2,1,0:T(8,128)S(1)}, f32[4,1,16]{2,0,1:T(4,128)S(1)}, f32[4,1,16]{2,0,1:T(4,128)S(1)}, f32[63,4,1,16]{3,1,2,0:T(4...) while((s32[]{:T(128)}, f32[4,1,16,128]{3,2,1,0:T(8,128)S(1)}, ...), condition=%wide.region_3.4_spmd, body=%wide.region_2.3_spmd.sunk | while | flops 25090 | bytes 102249 | solution.py:11
  226.8 0.8 fusion.37
  229.1 0.8 fusion.37
  233.6 0.8 fusion.37
  238.1 0.8 fusion.37
  240.4 0.8 fusion.37
  244.9 0.8 fusion.37
  247.2 0.8 fusion.37
  251.6 0.8 fusion.37
  256.1 0.8 fusion.37
  260.6 0.8 fusion.37
  262.9 0.8 fusion.37
  267.4 0.8 fusion.37
  274.1 0.8 fusion.37
  276.3 0.8 fusion.37
  278.6 0.8 fusion.37
  280.8 0.8 fusion.37
  285.3 0.8 fusion.37
  287.6 0.8 fusion.37
  289.8 0.8 fusion.37
  292.1 0.8 fusion.37
  296.6 0.8 fusion.37
  303.3 0.8 fusion.37
  305.6 0.8 fusion.37
  307.8 0.8 fusion.37
  316.9 0.8 fusion.37
  319.2 0.8 fusion.37
  323.7 0.8 fusion.37
  328.2 0.8 fusion.37
  332.7 0.8 fusion.37
  334.9 0.8 fusion.37
  337.1 0.8 fusion.37
  339.4 0.8 fusion.37
  341.6 0.8 fusion.37
  348.4 0.8 fusion.37
  350.7 0.8 fusion.37
  362.8 1.5 fusion.17
  364.3 10.0 %psum.28 = f32[4,256]{1,0:T(4,128)S(1)} all-reduce(f32[4,256]{1,0:T(4,128)S(1)} %fusion.17), channel_id=1, replica_groups=mesh['kvp'=64,'tp'=8] {'tp'}, use_global_device_ids=true, to_apply=%region_4.5 | all-reduce | flops 1024 | bytes 8192 | tf_op jit(solution)/shard_map/psum | solution.py:56
  374.4 140.6 %psum.29 = f32[4]{0:T(128)S(1)} all-reduce(f32[4]{0:T(128)S(1)} %multiply_reduce_fusion), channel_id=1, replica_groups=mesh['kvp'=64,'tp'=8] {'kvp'}, use_global_device_ids=true, to_apply=%region_6.7 | all-reduce | flops 4 | bytes 32 | tf_op jit(solution)/shard_map/psum | solution.py:57
  515.6 1.0 fusion.25
  516.6 1.0 fusion.24
  517.6 253.4 %all-reduce.3.cloned.1.call-done = (f32[4,3328]{1,0:T(4,128)}, f32[4,3328]{1,0:T(4,128)}) async-done(((f32[4,3328]{1,0:T(4,128)}, f32[4,3328]{1,0:T(4,128)}), (f32[4,3328]{1,0:T(4,128)}, f32[4,3328]{1,0:T(4,128)})) %all-reduce.3.cloned.1.call-update) | async-done | bytes 106512 | tf_op jit(solution)/shard_map/psum | solution.py:62
  771.0 1.5 fusion.12
  (242 shorter events, 114.8 us)
Async XLA Ops:
  7.2 508.5 %copy-start = (bf16[256,3328]{1,0:T(8,128)(2,1)S(1)}, bf16[256,3328]{1,0:T(8,128)(2,1)}, u32[]{:S(2)}) copy-start(bf16[256,3328]{1,0:T(8,128)(2,1)} %param.19) | copy-start | bytes 5111812
  7.2 209.9 %all-gather.7.cloned.1.call-start = ((), (), s32[]{:S(2)}) async-start(), calls=%async_computation | async-start | bytes 2129920 | tf_op jit(solution)/shard_map/all_gather | solution.py:8
  11.1 759.9 %all-reduce.3.cloned.1.call-start = ((), (), s32[]{:S(2)}) async-start(), calls=%async_computation.1 | async-start | bytes 212992 | tf_op jit(solution)/shard_map/psum | solution.py:62
  220.9 153.4 %copy-start.2 = (bf16[4,256]{1,0:T(4,128)(2,1)S(1)}, bf16[4,256]{1,0:T(4,128)(2,1)}, u32[]{:S(2)}) copy-start(bf16[4,256]{1,0:T(4,128)(2,1)} %param.16) | copy-start | bytes 6148
  220.9 294.1 %copy-start.3 = (f32[256]{0:T(256)S(1)}, f32[256]{0:T(256)}, u32[]{:S(2)}) copy-start(f32[256]{0:T(256)} %param.17) | copy-start | bytes 3076
  220.9 295.7 %copy-start.1 = (bf16[256,3328]{1,0:T(8,128)(2,1)S(1)}, bf16[256,3328]{1,0:T(8,128)(2,1)}, u32[]{:S(2)}) copy-start(bf16[256,3328]{1,0:T(8,128)(2,1)} %param.18) | copy-start | bytes 5111812
Sparse Core Ops, SparseCore 0:
  11.2 145.4 all-gather.6
  517.7 253.2 all-reduce.2
where the time goes:
time: 787 us; the launch traced here: 779 us
  blocking collectives  355 us (45%)
  waiting for transfers between devices  253 us (32%)
  other arithmetic  144 us (18%)
  between operations  14.1 us (2%)
    psum x1, waiting for transfers between devices, local(): gate_sum, up_sum = lax.psum((gate_part, up_part), 'kvp')  253 us
    all_gather x2, blocking collectives, combined_all(): pieces = jax.tree.map(lambda part: lax.all_gather(part, axis), value)  204 us
    psum x1, blocking collectives, local(): squares = lax.psum(jnp.sum(mixed * mixed, axis=1), 'kvp')  141 us
    add x63, other arithmetic, join_parts(): left_out * left_factor[..., None] + right_out * right_factor[..., None]  53.2 us
    add x63, other arithmetic, join_parts(): left_sum * left_factor + right_sum * right_factor  44.1 us
    mul x63, other arithmetic, join_parts(): left_out * left_factor[..., None] + right_out * right_factor[..., None]  42.9 us
  transfers between devices with their start and end apart: 2, of which 1 were waited for; matrix products, arithmetic and copies ran while one was open for 0% of the time, Pallas kernels for 0%

commit v1 on v0

v1 whole, which is shorter than its diff:
```python
import jax
import jax.numpy as jnp
from jax import lax
from jax.sharding import Mesh
from jax.sharding import PartitionSpec as P

NEAR = 8
LANES = 128


def spread(block, axis):
    count = lax.axis_size(axis)
    copies = jnp.broadcast_to(block[None], (count,) + block.shape)
    return lax.all_to_all(copies, axis, 0, 0, tiled=True)


def split_pair(value):
    high = value.astype(jnp.bfloat16)
    low = (value - high.astype(jnp.float32)).astype(jnp.bfloat16)
    return high, low


def pack(out, peak, total):
    stats = jnp.stack(split_pair(peak) + split_pair(total))
    stats = jnp.pad(stats, ((0, 12), (0, LANES - stats.shape[1])))
    return jnp.concatenate([out.astype(jnp.bfloat16), stats])


def combine(blocks):
    pairs = blocks.shape[1] - 16
    out = blocks[:, :pairs].astype(jnp.float32)
    stats = blocks[:, pairs:, :pairs].astype(jnp.float32)
    peaks = stats[:, 0] + stats[:, 1]
    totals = stats[:, 2] + stats[:, 3]
    peak = jnp.max(peaks, axis=0)
    factor = jnp.exp(peaks - peak[None])
    return jnp.sum(out * factor[..., None], axis=0), peak, jnp.sum(totals * factor, axis=0)


def local(
    query, key_cache, value_cache, lengths, out_weight, residual, norm_gain, gate_weight, up_weight
):
    rows, heads, head_dim = query.shape
    span = key_cache.shape[2]
    scores = jnp.einsum(
        "rgd,rpd->rgp", query, key_cache[:, 0], preferred_element_type=jnp.float32
    ) * head_dim ** (-0.5)
    block = lax.axis_index("far") * lax.axis_size("near") + lax.axis_index("near")
    positions = block * span + jnp.arange(span, dtype=jnp.int32)
    is_valid = (positions[None, :] < lengths[:, None])[:, None, :]
    masked = jnp.where(is_valid, scores, -1e30)
    high, low = split_pair(jnp.max(masked, axis=-1))
    peak = high.astype(jnp.float32) + low.astype(jnp.float32)
    weights = jnp.where(is_valid, jnp.exp(masked - peak[..., None]), 0.0)
    total = jnp.sum(weights, axis=-1)
    out = jnp.einsum(
        "rgp,rpd->rgd", weights.astype(jnp.bfloat16), value_cache[:, 0],
        preferred_element_type=jnp.float32,
    )
    state = (out.reshape(rows * heads, head_dim), peak.reshape(-1), total.reshape(-1))
    state = combine(spread(pack(*state), "near"))
    out, _, total = combine(spread(pack(*state), "far"))
    attention = (out / total[:, None]).astype(jnp.bfloat16).reshape(rows, heads * head_dim)
    projected = jnp.dot(attention, out_weight, preferred_element_type=jnp.float32)
    mixed = residual.astype(jnp.float32) + jnp.sum(spread(projected, "tp"), axis=0)
    squares = jnp.sum(mixed * mixed, axis=1)
    scaled = (mixed * norm_gain).astype(jnp.bfloat16)
    gate_part = jnp.dot(scaled, gate_weight, preferred_element_type=jnp.float32)
    up_part = jnp.dot(scaled, up_weight, preferred_element_type=jnp.float32)
    width = gate_part.shape[1]
    halves = NEAR // rows
    deep = width // halves // LANES
    tail = 32 - 2 * deep - 2

    def ending(value):
        pair = jnp.stack(split_pair(value), axis=-1)[..., None]
        pair = jnp.broadcast_to(pair, pair.shape[:-1] + (LANES,))
        return jnp.pad(pair, ((0, 0),) * (pair.ndim - 2) + ((0, tail), (0, 0)))

    terms = jnp.concatenate(
        [
            gate_part.astype(jnp.bfloat16).reshape(NEAR, deep, LANES),
            up_part.astype(jnp.bfloat16).reshape(NEAR, deep, LANES),
            ending(jnp.repeat(squares, halves)),
        ],
        axis=1,
    )
    terms = lax.all_to_all(terms, "near", 0, 0, tiled=True)
    terms = jnp.sum(terms.astype(jnp.float32), axis=0)
    squares = (terms[2 * deep] + terms[2 * deep + 1])[0]
    terms = jnp.concatenate([terms[: 2 * deep].astype(jnp.bfloat16), ending(squares)])
    terms = jnp.sum(spread(terms, "far").astype(jnp.float32), axis=0)
    squares = terms[2 * deep] + terms[2 * deep + 1]
    features = mixed.shape[1] * lax.axis_size("far") * lax.axis_size("near")
    inv_rms = lax.rsqrt(squares / features + 1e-05)
    gate_sum = terms[:deep] * inv_rms
    up_sum = terms[deep : 2 * deep] * inv_rms
    hidden = (jax.nn.silu(gate_sum) * up_sum).astype(jnp.bfloat16)
    hidden = spread(hidden, "near").reshape(rows, width)
    return (mixed.astype(jnp.bfloat16), hidden)


def solution(mesh):
    far = mesh.shape["kvp"] // NEAR
    devices = mesh.devices.reshape(far, NEAR, mesh.shape["tp"])
    inner = Mesh(devices, ("far", "near", "tp"))
    kvp = ("far", "near")
    placed = (
        P(None, "tp", None),
        P(None, "tp", kvp, None),
        P(None, "tp", kvp, None),
        P(),
        P("tp", kvp),
        P(None, kvp),
        P(kvp),
        P(kvp, "tp"),
        P(kvp, "tp"),
    )
    return jax.shard_map(
        local,
        mesh=inner,
        in_specs=placed,
        out_specs=(P(None, kvp), P(None, "tp")),
        check_vma=False,
    )
```

time: 787 us -> 94.7 us (0.12)
  blocking collectives: 355 us -> 84.7 us
  waiting for transfers between devices: 253 us -> 0 us
  other arithmetic: 144 us -> 2.48 us
  between operations: 14.1 us -> 0.93 us
    psum x1 -> x0, waiting for transfers between devices: 253 us -> none  [local(): gate_sum, up_sum = lax.psum((gate_part, up_part), 'kvp')]
    all_gather x2 -> x0, blocking collectives: 204 us -> none  [combined_all(): pieces = jax.tree.map(lambda part: lax.all_gather(part, axis), value)]
    psum x2 -> x0, blocking collectives: 151 us -> none  [the longest x1 141 us: local(): squares = lax.psum(jnp.sum(mixed * mixed, axis=1), 'kvp')]
    add x127 -> x3, other arithmetic: 97.3 us -> 0.01 us  [the longest x1 0.01 us: local(): squares = (terms[2 * deep] + terms[2 * deep + 1])[0]]
    all_to_all x0 -> x6, blocking collectives: none -> 84.7 us  [the longest x5 75.1 us: spread(): return lax.all_to_all(copies, axis, 0, 0, tiled=True)]
    mul x63 -> x1, other arithmetic: 42.9 us -> 0.01 us  [local(): gate_sum = terms[:deep] * inv_rms]
  transfers between devices with their start and end apart: 2 -> 0, of which waited for: 1 -> 0; matrix products, arithmetic and copies ran while one was open for 0% -> 0% of each run, Pallas kernels for 0% -> 0%
where the time goes in v1:
time: 94.7 us; the launch traced here: 94.3 us
  blocking collectives  84.7 us (89%)
  matrix products  4.69 us (5%)
  other arithmetic  2.48 us (3%)
  local copies, waits for them, and re-layouts  1.58 us (2%)
    all_to_all x5, blocking collectives, spread(): return lax.all_to_all(copies, axis, 0, 0, tiled=True)  75.1 us
    all_to_all x1, blocking collectives, local(): terms = lax.all_to_all(terms, 'near', 0, 0, tiled=True)  9.52 us

profile of v1, /device:TPU:2, one launch (start us, length us, event | category | flops | bytes accessed | tf_op | source)
XLA Modules:
  0.0 94.3 jit_solution(2119980109259898126)
XLA Ops:
  0.6 0.0 copy-start
  0.7 0.9 broadcast_compare_fusion
  1.5 1.2 %fusion.55 = (f32[4,16]{1,0:T(4,128)S(1)}, f32[4,16,256]{2,1,0:T(8,128)S(1)}) fusion(bf16[4,16,128]{2,1,0:T(8,128)(2,1)} %param.9, bf16[4,1,256,128]{3,2,1,0:T(8,128)(2,1)} %param.10, pred[4,256]{1,0:T(4,128)(4,1)S(1)} %broadcast_compare_fusion), kind=kOutput, calls=%fused_computation.102 | convolution fusion | flops 4243392 | bytes 345344 | tf_op jit(solution)/shard_map/rgd,rpd->rgp/dot_general | solution.py:45
  2.7 0.1 reduce_max.32
  2.8 0.2 fusion.5
  3.0 0.0 copy-start.2
  3.0 0.0 copy-start.3
  3.0 1.2 %convolution_convert_fusion.2 = bf16[4,16,128]{2,1,0:T(8,128)(2,1)S(1)} fusion(bf16[4,1,256,128]{3,2,1,0:T(8,128)(2,1)} %param.11, f32[4,16,256]{2,1,0:T(8,128)S(1)} %get-tuple-element.22, f32[4,16]{1,0:T(4,128)S(1)} %convert_add_fusion.1, pred[4,256]{1,0:T(4,128)(4,1)S(1)} %broadcast_compare_fusion), kind=kOutput, calls=%fused_computation.4 | convolution fusion | flops 4251648 | bytes 345344 | tf_op jit(solution)/shard_map/rgp,rpd->rgd/dot_general | solution.py:56
  4.2 0.1 reshape.271
  4.4 12.4 %all_to_all.30 = bf16[8,80,128]{2,1,0:T(8,128)(2,1)S(1)} all-to-all(bf16[8,80,128]{2,1,0:T(8,128)(2,1)S(1)} %broadcast_in_dim.35), channel_id=1, replica_groups=mesh['far'=8,'near'=8,'tp'=8] {'near'}, dimensions={0} | all-to-all | bytes 327680 | tf_op jit(solution)/shard_map/all_to_all | solution.py:14
  16.9 0.1 multiply_reduce_fusion.1
  17.1 28.9 %all_to_all.31 = bf16[8,80,128]{2,1,0:T(8,128)(2,1)S(1)} all-to-all(bf16[8,80,128]{2,1,0:T(8,128)(2,1)S(1)} %broadcast_in_dim.36), channel_id=1, replica_groups=mesh['far'=8,'near'=8,'tp'=8] {'far'}, dimensions={0} | all-to-all | bytes 327680 | tf_op jit(solution)/shard_map/all_to_all | solution.py:14
  46.0 0.0 copy-start.1
  46.0 0.1 multiply_reduce_fusion
  46.2 0.1 div.23
  46.3 0.1 broadcast_bitcast_fusion
  46.3 1.6 %fusion.12 = f32[4,256]{1,0:T(4,128)S(1)} fusion(bf16[2048,256]{1,0:T(8,128)(2,1)} %param.13, f32[4,2048]{1,0:T(4,128)S(1)} %reduce_sum.90, f32[1,4,16,128]{3,2,1,0:T(8,128)S(1)} %broadcast_bitcast_fusion), kind=kOutput, calls=%fused_computation.26 | convolution fusion | flops 4210688 | bytes 1118208 | tf_op jit(solution)/shard_map/dot_general | solution.py:64
  47.9 8.6 %all_to_all.32 = f32[8,4,256]{2,1,0:T(4,128)S(1)} all-to-all(f32[8,4,256]{2,1,0:T(4,128)S(1)} %broadcast_in_dim.37), channel_id=1, replica_groups=mesh['far'=8,'near'=8,'tp'=8] {'tp'}, dimensions={0} | all-to-all | bytes 65536 | tf_op jit(solution)/shard_map/all_to_all | solution.py:14
  56.6 0.0 copy-done.2
  56.6 0.0 copy-done.3
  56.6 0.7 multiply_convert_fusion
  57.3 0.1 broadcast_in_dim.38
  57.4 0.1 reshape.274
  57.5 0.1 copy.31
  57.6 0.0 copy-done
  57.6 0.3 convolution_convert_fusion
  58.0 0.0 copy-done.1
  58.0 0.3 convolution_convert_fusion.1
  58.4 0.1 broadcast_in_dim.39
  58.5 9.5 %all_to_all.33 = bf16[8,32,128]{2,1,0:T(8,128)(2,1)S(1)} all-to-all(bf16[8,32,128]{2,1,0:T(8,128)(2,1)S(1)} %fusion.4), channel_id=1, replica_groups=mesh['far'=8,'near'=8,'tp'=8] {'near'}, dimensions={0} | all-to-all | bytes 131072 | tf_op jit(solution)/shard_map/all_to_all | solution.py:88
  68.1 0.1 fusion.43
  68.2 0.1 pad.23.clone
  68.3 0.1 pad_maximum_fusion.2
  68.4 16.2 %all_to_all.34 = bf16[8,32,128]{2,1,0:T(8,128)(2,1)S(1)} all-to-all(bf16[8,32,128]{2,1,0:T(8,128)(2,1)S(1)} %broadcast_in_dim.40), channel_id=1, replica_groups=mesh['far'=8,'near'=8,'tp'=8] {'far'}, dimensions={0} | all-to-all | bytes 131072 | tf_op jit(solution)/shard_map/all_to_all | solution.py:14
  84.7 9.0 %all_to_all.35 = bf16[8,13,128]{2,1,0:T(8,128)(2,1)S(1)} all-to-all(bf16[8,13,128]{2,1,0:T(8,128)(2,1)S(1)} %broadcast_in_dim.41), channel_id=1, replica_groups=mesh['far'=8,'near'=8,'tp'=8] {'near'}, dimensions={0} | all-to-all | bytes 53248 | tf_op jit(solution)/shard_map/all_to_all | solution.py:14
  93.7 0.6 reshape.275
  (37 shorter events, 0.5 us)
Async XLA Ops:
  0.6 56.9 %copy-start = (bf16[256,3328]{1,0:T(8,128)(2,1)S(1)}, bf16[256,3328]{1,0:T(8,128)(2,1)}, u32[]{:S(2)}) copy-start(bf16[256,3328]{1,0:T(8,128)(2,1)} %param.17) | copy-start | bytes 5111812
  3.0 53.6 %copy-start.2 = (bf16[4,256]{1,0:T(4,128)(2,1)S(1)}, bf16[4,256]{1,0:T(4,128)(2,1)}, u32[]{:S(2)}) copy-start(bf16[4,256]{1,0:T(4,128)(2,1)} %param.14) | copy-start | bytes 6148
  3.0 53.6 %copy-start.3 = (f32[256]{0:T(256)S(1)}, f32[256]{0:T(256)}, u32[]{:S(2)}) copy-start(f32[256]{0:T(256)} %param.15) | copy-start | bytes 3076
  46.0 12.0 %copy-start.1 = (bf16[256,3328]{1,0:T(8,128)(2,1)S(1)}, bf16[256,3328]{1,0:T(8,128)(2,1)}, u32[]{:S(2)}) copy-start(bf16[256,3328]{1,0:T(8,128)(2,1)} %param.16) | copy-start | bytes 5111812

commit v2 on v1

v2 whole, which is shorter than its diff:
```python
import jax
import jax.numpy as jnp
from jax import lax
from jax.experimental import pallas as pl
from jax.experimental.pallas import tpu as pltpu
from jax.sharding import Mesh
from jax.sharding import PartitionSpec as P

NEAR = 8
LANES = 128


def spread(block, axis):
    count = lax.axis_size(axis)
    copies = jnp.broadcast_to(block[None], (count,) + block.shape)
    return lax.all_to_all(copies, axis, 0, 0, tiled=True)


def split_pair(value):
    high = lax.reduce_precision(value, 8, 7)
    low = lax.reduce_precision(value - high, 8, 7)
    return high, low


def pack(out, stats):
    return jnp.concatenate([out.astype(jnp.bfloat16), stats.astype(jnp.bfloat16)])


def combine(blocks):
    pairs = blocks.shape[1] - 8
    out = blocks[:, :pairs].astype(jnp.float32)
    stats = blocks[:, pairs:, :pairs].astype(jnp.float32)
    peaks = stats[:, 0] + stats[:, 1]
    totals = stats[:, 2] + stats[:, 3]
    peak = jnp.max(peaks, axis=0)
    factor = jnp.exp(peaks - peak[None])
    total = jnp.sum(totals * factor, axis=0)
    return jnp.sum(out * factor[..., None], axis=0), peak, total


def stacked(peak, total):
    stats = jnp.stack(split_pair(peak) + split_pair(total))
    return jnp.pad(stats, ((0, 4), (0, LANES - stats.shape[1])))


def halves_of(value):
    high = value.astype(jnp.bfloat16).astype(jnp.float32)
    return high, value - high


def attend(
    lengths_hbm, query_hbm, key_hbm, value_hbm, *others,
):
    count = (len(others) - 7) // 2
    out_ref, stats_ref, *fetched = others[count : 2 * count + 2]
    lengths_ref, query_ref, key_ref, value_ref, arrived = others[2 * count + 2 :]
    sources = (lengths_hbm, query_hbm, key_hbm, value_hbm, *others[:count])
    targets = (lengths_ref, query_ref, key_ref, value_ref, *fetched)
    copies = [
        pltpu.make_async_copy(source, target, arrived.at[at])
        for at, (source, target) in enumerate(zip(sources, targets))
    ]
    for copy in copies:
        copy.start()
    rows, heads, head_dim = query_ref.shape
    span = key_ref.shape[2]
    block = lax.axis_index("far") * NEAR + lax.axis_index("near")
    positions = block * span + lax.broadcasted_iota(jnp.int32, (heads, span), 1)
    lane = lax.broadcasted_iota(jnp.int32, (rows * heads, LANES), 1)
    for copy in copies[:3]:
        copy.wait()
    scores = [
        lax.dot_general(
            query_ref[row], key_ref[row, 0], (((1,), (1,)), ((), ())),
            preferred_element_type=jnp.float32,
        )
        for row in range(rows)
    ]
    live = jnp.concatenate([positions < lengths_ref[row] for row in range(rows)])
    masked = jnp.where(live, jnp.concatenate(scores) * head_dim ** (-0.5), -1e30)
    top = jnp.max(masked, axis=1, keepdims=True)
    high, low = halves_of(top)
    low = low.astype(jnp.bfloat16).astype(jnp.float32)
    weights = jnp.where(live, jnp.exp(masked - (high + low)), 0.0)
    rounded = weights.astype(jnp.bfloat16)
    copies[3].wait()
    for row in range(rows):
        out_ref[row] = jnp.dot(
            rounded[row * heads : (row + 1) * heads], value_ref[row, 0],
            preferred_element_type=jnp.float32,
        ).astype(jnp.bfloat16)
    total_high, total_low = halves_of(jnp.sum(weights, axis=1, keepdims=True))
    stats = jnp.where(lane == 0, high, jnp.where(lane == 1, low, 0.0))
    stats = jnp.where(lane == 2, total_high, jnp.where(lane == 3, total_low, stats))
    empty = jnp.zeros((LANES - rows * heads, LANES), jnp.float32)
    stats_ref[...] = jnp.concatenate([stats, empty]).T[:8]
    for copy in copies[4:]:
        copy.wait()


def project(blocks_ref, weight_ref, out_ref, attention_ref):
    count = blocks_ref.shape[0]
    pairs = attention_ref.shape[0]
    rows = out_ref.shape[0]
    heads = pairs // rows
    blocks = [blocks_ref[at].astype(jnp.float32) for at in range(count)]
    stats = [block[pairs : pairs + 8] for block in blocks]
    peaks = [stat[0:1] + stat[1:2] for stat in stats]
    peak = peaks[0]
    for other in peaks[1:]:
        peak = jnp.maximum(peak, other)
    factors = [jnp.exp(other - peak) for other in peaks]
    lane = lax.broadcasted_iota(jnp.int32, (1, LANES), 1)
    total = jnp.where(lane < pairs, 0.0, 1.0)
    for factor, stat in zip(factors, stats):
        total = total + factor * (stat[2:3] + stat[3:4])
    factors = jnp.concatenate([factor / total for factor in factors])
    empty = jnp.zeros((LANES - count, LANES), jnp.float32)
    columns = jnp.concatenate([factors, empty]).T
    attention = blocks[0][:pairs] * columns[:pairs, 0:1]
    for at in range(1, count):
        attention = attention + blocks[at][:pairs] * columns[:pairs, at : at + 1]
    attention_ref[...] = attention
    attention = jnp.concatenate(
        [attention_ref[pl.ds(head, rows, stride=heads), :] for head in range(heads)], axis=1
    ).astype(jnp.bfloat16)
    out_ref[...] = jnp.dot(attention, weight_ref[...], preferred_element_type=jnp.float32)


def feed(terms_ref, residual_ref, gain_ref, gate_ref, up_ref, mixed_ref, wide_ref):
    mixed = residual_ref[...].astype(jnp.float32)
    for at in range(terms_ref.shape[0]):
        mixed = mixed + terms_ref[at]
    mixed_ref[...] = mixed
    rows = mixed.shape[0]
    halves = NEAR // rows
    deep = gate_ref.shape[1] // halves // LANES
    squares = jnp.sum(mixed * mixed, axis=1, keepdims=True)
    high, low = halves_of(jnp.broadcast_to(squares, (rows, LANES)))
    wide_ref[...] = jnp.zeros_like(wide_ref)
    for half in range(halves):
        wide_ref[pl.ds(half, rows, stride=halves), 2 * deep, :] = high
        wide_ref[pl.ds(half, rows, stride=halves), 2 * deep + 1, :] = low
    scaled = (mixed * gain_ref[...]).astype(jnp.bfloat16)
    for first, weight_ref in ((0, gate_ref), (deep, up_ref)):
        terms = jnp.dot(scaled, weight_ref[...], preferred_element_type=jnp.float32)
        for half in range(halves):
            for at in range(deep):
                column = (half * deep + at) * LANES
                piece = terms[:, column : column + LANES]
                wide_ref[pl.ds(half, rows, stride=halves), first + at, :] = piece


def finish(mixed_ref, blocks_ref, stream_hbm, hidden_hbm, wide_ref, stream_ref, hidden_ref, sent):
    stream_ref[...] = mixed_ref[...].astype(jnp.bfloat16)
    first = pltpu.make_async_copy(stream_ref, stream_hbm, sent.at[0])
    first.start()
    rows = stream_ref.shape[0]
    halves = NEAR // rows
    deep = blocks_ref.shape[1]
    wide_ref[...] = blocks_ref[...].astype(jnp.float32)
    for half in range(halves):
        for at in range(deep):
            piece = wide_ref[pl.ds(half, rows, stride=halves), at, :]
            column = (half * deep + at) * LANES
            hidden_ref[:, column : column + LANES] = piece.astype(jnp.bfloat16)
    second = pltpu.make_async_copy(hidden_ref, hidden_hbm, sent.at[1])
    second.start()
    first.wait()
    second.wait()


def local(
    query, key_cache, value_cache, lengths, out_weight, residual, norm_gain, gate_weight, up_weight
):
    rows, heads, head_dim = query.shape
    vmem, hbm = pl.BlockSpec(memory_space=pltpu.VMEM), pl.BlockSpec(memory_space=pltpu.HBM)
    params = pltpu.CompilerParams(vmem_limit_bytes=16 * 2**20)
    sources = (lengths, query, key_cache, value_cache, up_weight)
    out, stats, up_weight = pl.pallas_call(
        attend,
        out_shape=(
            pltpu.VMEM((rows, heads, head_dim), jnp.bfloat16),
            pltpu.VMEM((8, LANES), jnp.float32),
            pltpu.VMEM(up_weight.shape, jnp.bfloat16),
        ),
        in_specs=[hbm] * len(sources),
        out_specs=(vmem,) * 3,
        scratch_shapes=[
            pltpu.SMEM(lengths.shape, jnp.int32),
            pltpu.VMEM(query.shape, jnp.bfloat16),
            pltpu.VMEM(key_cache.shape, jnp.bfloat16),
            pltpu.VMEM(value_cache.shape, jnp.bfloat16),
            pltpu.SemaphoreType.DMA((len(sources),)),
        ],
        compiler_params=params,
    )(*[pltpu.with_memory_space_constraint(source, pltpu.HBM) for source in sources])
    out = out.reshape(rows * heads, head_dim)
    out, peak, total = combine(spread(pack(out, stats), "near"))
    blocks = spread(pack(out, stacked(peak, total)), "far")
    block_width = out_weight.shape[1]
    projected = pl.pallas_call(
        project,
        out_shape=jax.ShapeDtypeStruct((rows, block_width), jnp.float32),
        in_specs=[vmem] * 2,
        out_specs=vmem,
        scratch_shapes=[pltpu.VMEM((rows * heads, head_dim), jnp.float32)],
        compiler_params=params,
    )(blocks, out_weight)
    width = gate_weight.shape[1]
    halves = NEAR // rows
    deep = width // halves // LANES
    tall = -(-(2 * deep + 2) // 16) * 16
    mixed, terms = pl.pallas_call(
        feed,
        out_shape=(
            pltpu.VMEM((rows, block_width), jnp.float32),
            pltpu.VMEM((NEAR, tall, LANES), jnp.float32),
        ),
        in_specs=[vmem] * 5,
        out_specs=(vmem,) * 2,
        compiler_params=params,
    )(spread(projected, "tp"), residual, norm_gain.reshape(1, -1), gate_weight, up_weight)

    terms = lax.all_to_all(terms.astype(jnp.bfloat16), "near", 0, 0, tiled=True)
    terms = jnp.sum(terms.astype(jnp.float32), axis=0)
    pair = jnp.stack(split_pair(terms[2 * deep] + terms[2 * deep + 1]))
    terms = jnp.concatenate([terms[: 2 * deep], pair, terms[2 * deep + 2 :]]).astype(jnp.bfloat16)
    terms = jnp.sum(spread(terms, "far").astype(jnp.float32), axis=0)
    features = block_width * lax.axis_size("far") * lax.axis_size("near")
    mean_square = (terms[2 * deep] + terms[2 * deep + 1]) / features
    inv_rms = lax.rsqrt(mean_square + 1e-05)
    gate_sum = terms[:deep] * inv_rms
    up_sum = terms[deep : 2 * deep] * inv_rms
    hidden = (jax.nn.silu(gate_sum) * up_sum).astype(jnp.bfloat16)
    blocks = spread(hidden, "near")
    return tuple(pl.pallas_call(
        finish,
        out_shape=(
            jax.ShapeDtypeStruct((rows, block_width), jnp.bfloat16),
            jax.ShapeDtypeStruct((rows, width), jnp.bfloat16),
        ),
        in_specs=[vmem] * 2,
        out_specs=(hbm, hbm),
        scratch_shapes=[
            pltpu.VMEM(blocks.shape, jnp.float32),
            pltpu.VMEM((rows, block_width), jnp.bfloat16),
            pltpu.VMEM((rows, width), jnp.bfloat16),
            pltpu.SemaphoreType.DMA((2,)),
        ],
        compiler_params=params,
    )(mixed, blocks))


def solution(mesh):
    far = mesh.shape["kvp"] // NEAR
    devices = mesh.devices.reshape(far, NEAR, mesh.shape["tp"])
    inner = Mesh(devices, ("far", "near", "tp"))
    kvp = ("far", "near")
    placed = (
        P(None, "tp", None),
        P(None, "tp", kvp, None),
        P(None, "tp", kvp, None),
        P(),
        P("tp", kvp),
        P(None, kvp),
        P(kvp),
        P(kvp, "tp"),
        P(kvp, "tp"),
    )
    return jax.shard_map(
        local,
        mesh=inner,
        in_specs=placed,
        out_specs=(P(None, kvp), P(None, "tp")),
        check_vma=False,
    )
```

time: 94.7 us -> 89.1 us (0.941)
  matrix products: 4.69 us -> 0 us
  Pallas kernels: 0 us -> 3.51 us
  other arithmetic: 2.48 us -> 0.32 us
  local copies, waits for them, and re-layouts: 1.58 us -> 0.1 us
    dot_general x5 -> x0, matrix products: 4.69 us -> none  [the longest x1 1.6 us: local(): jnp.dot(attention, out_weight, preferred_element_type=jnp.float32)]
    pallas_call x0 -> x4, Pallas kernels: none -> 3.51 us  [the longest x1 1.76 us: local(): pl.pallas_call(attend, out_shape=(pltpu.VMEM((rows, heads, head_dim), jnp...]
where the time goes in v2:
time: 89.1 us; the launch traced here: 88.8 us
  blocking collectives  84 us (94%)
  Pallas kernels  3.51 us (4%)
    all_to_all x5, blocking collectives, spread(): return lax.all_to_all(copies, axis, 0, 0, tiled=True)  75.1 us
    all_to_all x1, blocking collectives, local(): terms = lax.all_to_all(terms.astype(jnp.bfloat16), 'near', 0, 0, tiled=True)  8.92 us

profile of v2, /device:TPU:2, one launch (start us, length us, event | category | flops | bytes accessed | tf_op | source)
XLA Modules:
  0.0 88.8 jit_solution(15305918543603783808)
XLA Ops:
  0.6 0.0 copy-start.1
  0.6 1.8 %shard_map.104 = (bf16[4,16,128]{2,1,0:T(8,128)(2,1)S(1)}, f32[8,128]{1,0:T(8,128)S(1)}, bf16[256,3328]{1,0:T(8,128)(2,1)S(1)}) custom-call(s32[4]{0:T(128)} %lengths_hbm.1, bf16[4,16,128]{2,1,0:T(8,128)(2,1)} %query_hbm.1, bf16[4,1,256,128]{3,2,1,0:T(8,128)(2,1)} %key_hbm.1, bf16[4,1,256,128]{3,2,1,0:T(8,128)(2,1)} %value_hbm.1, bf16[256,3328]{1,0:T(8,128)(2,1)} %others_0_.1), custom_call_target="tpu_custom_call" | custom-call | tf_op jit(solution)/shard_map/pallas_call | solution.py:180
  2.4 0.0 copy-start
  2.4 0.0 copy-start.2
  2.4 0.0 copy-start.3
  2.5 12.4 %all_to_all.30 = bf16[8,72,128]{2,1,0:T(8,128)(2,1)S(1)} all-to-all(bf16[8,72,128]{2,1,0:T(8,128)(2,1)S(1)} %broadcast_in_dim.10), channel_id=1, replica_groups=mesh['far'=8,'near'=8,'tp'=8] {'near'}, dimensions={0} | all-to-all | bytes 294912 | tf_op jit(solution)/shard_map/all_to_all | solution.py:16
  15.0 0.1 multiply_reduce_fusion
  15.2 28.8 %all_to_all.31.blocks_ref = bf16[8,72,128]{2,1,0:T(8,128)(2,1)S(1)} all-to-all(bf16[8,72,128]{2,1,0:T(8,128)(2,1)S(1)} %broadcast_in_dim.11), channel_id=1, replica_groups=mesh['far'=8,'near'=8,'tp'=8] {'far'}, dimensions={0} | all-to-all | bytes 294912 | tf_op jit(solution)/shard_map/all_to_all | solution.py:16
  44.0 0.0 copy-done.1
  44.0 0.5 shard_map.105
  44.5 8.6 %all_to_all.32.terms_ref = f32[8,4,256]{2,1,0:T(4,128)S(1)} all-to-all(f32[8,4,256]{2,1,0:T(4,128)S(1)} %broadcast_in_dim.12), channel_id=1, replica_groups=mesh['far'=8,'near'=8,'tp'=8] {'tp'}, dimensions={0} | all-to-all | bytes 65536 | tf_op jit(solution)/shard_map/all_to_all | solution.py:16
  53.1 0.0 copy-done
  53.1 0.0 copy-done.2
  53.1 0.0 copy-done.3
  53.1 0.6 shard_map.106
  53.7 8.9 %all_to_all.33 = bf16[8,32,128]{2,1,0:T(8,128)(2,1)S(1)} all-to-all(bf16[8,32,128]{2,1,0:T(8,128)(2,1)S(1)} %convert_element_type.36), channel_id=1, replica_groups=mesh['far'=8,'near'=8,'tp'=8] {'near'}, dimensions={0} | all-to-all | bytes 131072 | tf_op jit(solution)/shard_map/all_to_all | solution.py:225
  62.7 16.3 %all_to_all.34 = bf16[8,32,128]{2,1,0:T(8,128)(2,1)S(1)} all-to-all(bf16[8,32,128]{2,1,0:T(8,128)(2,1)S(1)} %broadcast_in_dim.13), channel_id=1, replica_groups=mesh['far'=8,'near'=8,'tp'=8] {'far'}, dimensions={0} | all-to-all | bytes 131072 | tf_op jit(solution)/shard_map/all_to_all | solution.py:16
  79.1 9.0 %all_to_all.35.blocks_ref = bf16[8,13,128]{2,1,0:T(8,128)(2,1)S(1)} all-to-all(bf16[8,13,128]{2,1,0:T(8,128)(2,1)S(1)} %broadcast_in_dim.14), channel_id=1, replica_groups=mesh['far'=8,'near'=8,'tp'=8] {'near'}, dimensions={0} | all-to-all | bytes 53248 | tf_op jit(solution)/shard_map/all_to_all | solution.py:16
  88.1 0.7 shard_map.107
  (23 shorter events, 0.3 us)
Async XLA Ops:
  0.6 43.4 %copy-start.1 = (bf16[2048,256]{1,0:T(8,128)(2,1)S(1)}, bf16[2048,256]{1,0:T(8,128)(2,1)}, u32[]{:S(2)}) copy-start(bf16[2048,256]{1,0:T(8,128)(2,1)} %weight_ref.1) | copy-start | bytes 3145732
  2.4 50.7 %copy-start = (bf16[256,3328]{1,0:T(8,128)(2,1)S(1)}, bf16[256,3328]{1,0:T(8,128)(2,1)}, u32[]{:S(2)}) copy-start(bf16[256,3328]{1,0:T(8,128)(2,1)} %gate_ref.1) | copy-start | bytes 5111812
  2.4 50.7 %copy-start.2 = (bf16[4,256]{1,0:T(4,128)(2,1)S(1)}, bf16[4,256]{1,0:T(4,128)(2,1)}, u32[]{:S(2)}) copy-start(bf16[4,256]{1,0:T(4,128)(2,1)} %residual_ref.1) | copy-start | bytes 6148
  2.4 50.7 %copy-start.3 = (f32[256]{0:T(256)S(1)}, f32[256]{0:T(256)}, u32[]{:S(2)}) copy-start(f32[256]{0:T(256)} %param.15) | copy-start | bytes 3076

commit v3 on v2

--- a/solution.py
+++ b/solution.py
@@ -3,17 +3,27 @@
 from jax import lax
 from jax.experimental import pallas as pl
 from jax.experimental.pallas import tpu as pltpu
-from jax.sharding import Mesh
 from jax.sharding import PartitionSpec as P
 
 NEAR = 8
 LANES = 128
 
 
-def spread(block, axis):
-    count = lax.axis_size(axis)
-    copies = jnp.broadcast_to(block[None], (count,) + block.shape)
-    return lax.all_to_all(copies, axis, 0, 0, tiled=True)
+def teams(count):
+    near = []
+    for first in range(0, count, NEAR):
+        turn = NEAR // 2 if 2 * first >= count else 0
+        near.append([first + (at ^ turn) for at in range(NEAR)])
+    return near, [list(far) for far in zip(*near)]
+
+
+def exchange(blocks, axis, groups=None):
+    return lax.all_to_all(blocks, axis, 0, 0, axis_index_groups=groups, tiled=True)
+
+
+def spread(block, axis, groups=None):
+    count = len(groups[0]) if groups else lax.axis_size(axis)
+    return exchange(jnp.broadcast_to(block[None], (count,) + block.shape), axis, groups)
 
 
 def split_pair(value):
@@ -64,7 +74,7 @@
         copy.start()
     rows, heads, head_dim = query_ref.shape
     span = key_ref.shape[2]
-    block = lax.axis_index("far") * NEAR + lax.axis_index("near")
+    block = lax.axis_index("kvp")
     positions = block * span + lax.broadcasted_iota(jnp.int32, (heads, span), 1)
     lane = lax.broadcasted_iota(jnp.int32, (rows * heads, LANES), 1)
     for copy in copies[:3]:
@@ -174,6 +184,7 @@
     query, key_cache, value_cache, lengths, out_weight, residual, norm_gain, gate_weight, up_weight
 ):
     rows, heads, head_dim = query.shape
+    near, far = teams(lax.axis_size("kvp"))
     vmem, hbm = pl.BlockSpec(memory_space=pltpu.VMEM), pl.BlockSpec(memory_space=pltpu.HBM)
     params = pltpu.CompilerParams(vmem_limit_bytes=16 * 2**20)
     sources = (lengths, query, key_cache, value_cache, up_weight)
@@ -196,8 +207,8 @@
         compiler_params=params,
     )(*[pltpu.with_memory_space_constraint(source, pltpu.HBM) for source in sources])
     out = out.reshape(rows * heads, head_dim)
-    out, peak, total = combine(spread(pack(out, stats), "near"))
-    blocks = spread(pack(out, stacked(peak, total)), "far")
+    out, peak, total = combine(spread(pack(out, stats), "kvp", near))
+    blocks = spread(pack(out, stacked(peak, total)), "kvp", far)
     block_width = out_weight.shape[1]
     projected = pl.pallas_call(
         project,
@@ -222,18 +233,18 @@
         compiler_params=params,
     )(spread(projected, "tp"), residual, norm_gain.reshape(1, -1), gate_weight, up_weight)
 
-    terms = lax.all_to_all(terms.astype(jnp.bfloat16), "near", 0, 0, tiled=True)
+    terms = exchange(terms.astype(jnp.bfloat16), "kvp", near)
     terms = jnp.sum(terms.astype(jnp.float32), axis=0)
     pair = jnp.stack(split_pair(terms[2 * deep] + terms[2 * deep + 1]))
     terms = jnp.concatenate([terms[: 2 * deep], pair, terms[2 * deep + 2 :]]).astype(jnp.bfloat16)
-    terms = jnp.sum(spread(terms, "far").astype(jnp.float32), axis=0)
-    features = block_width * lax.axis_size("far") * lax.axis_size("near")
+    terms = jnp.sum(spread(terms, "kvp", far).astype(jnp.float32), axis=0)
+    features = block_width * lax.axis_size("kvp")
     mean_square = (terms[2 * deep] + terms[2 * deep + 1]) / features
     inv_rms = lax.rsqrt(mean_square + 1e-05)
     gate_sum = terms[:deep] * inv_rms
     up_sum = terms[deep : 2 * deep] * inv_rms
     hidden = (jax.nn.silu(gate_sum) * up_sum).astype(jnp.bfloat16)
-    blocks = spread(hidden, "near")
+    blocks = spread(hidden, "kvp", near)
     return tuple(pl.pallas_call(
         finish,
         out_shape=(
@@ -253,25 +264,21 @@
 
 
 def solution(mesh):
-    far = mesh.shape["kvp"] // NEAR
-    devices = mesh.devices.reshape(far, NEAR, mesh.shape["tp"])
-    inner = Mesh(devices, ("far", "near", "tp"))
-    kvp = ("far", "near")
     placed = (
         P(None, "tp", None),
-        P(None, "tp", kvp, None),
-        P(None, "tp", kvp, None),
+        P(None, "tp", "kvp", None),
+        P(None, "tp", "kvp", None),
         P(),
-        P("tp", kvp),
-        P(None, kvp),
-        P(kvp),
-        P(kvp, "tp"),
-        P(kvp, "tp"),
+        P("tp", "kvp"),
+        P(None, "kvp"),
+        P("kvp"),
+        P("kvp", "tp"),
+        P("kvp", "tp"),
     )
     return jax.shard_map(
         local,
-        mesh=inner,
+        mesh=mesh,
         in_specs=placed,
-        out_specs=(P(None, kvp), P(None, "tp")),
+        out_specs=(P(None, "kvp"), P(None, "tp")),
         check_vma=False,
     )

time: 89.1 us -> 86.9 us (0.975)
  blocking collectives: 84 us -> 81.8 us
    all_to_all x6, blocking collectives: 84 us -> 81.8 us  [exchange(): lax.all_to_all(blocks, axis, 0, 0, axis_index_groups=groups, tiled=True)]
where the time goes in v3:
time: 86.9 us; the launch traced here: 86.5 us
  blocking collectives  81.8 us (94%)
  Pallas kernels  3.51 us (4%)
    all_to_all x6, blocking collectives, exchange(): lax.all_to_all(blocks, axis, 0, 0, axis_index_groups=groups, tiled=True)  81.8 us
    pallas_call x1, Pallas kernels, local(): pl.pallas_call(attend, out_shape=(pltpu.VMEM((rows, heads, head_dim), jnp...  1.76 us

profile of v3, /device:TPU:2, one launch (start us, length us, event | category | flops | bytes accessed | tf_op | source)
XLA Modules:
  0.0 86.5 jit_solution(12967366438253328030)
XLA Ops:
  0.6 0.0 copy-start.1
  0.6 1.8 %shard_map.104 = (bf16[4,16,128]{2,1,0:T(8,128)(2,1)S(1)}, f32[8,128]{1,0:T(8,128)S(1)}, bf16[256,3328]{1,0:T(8,128)(2,1)S(1)}) custom-call(s32[4]{0:T(128)} %lengths_hbm.1, bf16[4,16,128]{2,1,0:T(8,128)(2,1)} %query_hbm.1, bf16[4,1,256,128]{3,2,1,0:T(8,128)(2,1)} %key_hbm.1, bf16[4,1,256,128]{3,2,1,0:T(8,128)(2,1)} %value_hbm.1, bf16[256,3328]{1,0:T(8,128)(2,1)} %others_0_.1), custom_call_target="tpu_custom_call" | custom-call | tf_op jit(solution)/shard_map/pallas_call | solution.py:191
  2.4 0.0 copy-start
  2.4 0.0 copy-start.2
  2.4 0.0 copy-start.3
  2.5 12.4 %all_to_all.30 = bf16[8,72,128]{2,1,0:T(8,128)(2,1)S(1)} all-to-all(bf16[8,72,128]{2,1,0:T(8,128)(2,1)S(1)} %broadcast_in_dim.10), channel_id=1, replica_groups={{0,8,16,24,32,40,48,56},{64,72,80,88,96,104,112,120},{128,136,144,152,1..., dimensions={0} | all-to-all | bytes 294912 | tf_op jit(solution)/shard_map/all_to_all | solution.py:21
  15.0 0.1 multiply_reduce_fusion
  15.2 28.4 %all_to_all.31.blocks_ref = bf16[8,72,128]{2,1,0:T(8,128)(2,1)S(1)} all-to-all(bf16[8,72,128]{2,1,0:T(8,128)(2,1)S(1)} %broadcast_in_dim.11), channel_id=1, replica_groups={{0,64,128,192,288,352,416,480},{8,72,136,200,296,360,424,488},{16,80,14..., dimensions={0} | all-to-all | bytes 294912 | tf_op jit(solution)/shard_map/all_to_all | solution.py:21
  43.6 0.0 copy-done.1
  43.6 0.5 shard_map.105
  44.1 8.6 %all_to_all.32.terms_ref = f32[8,4,256]{2,1,0:T(4,128)S(1)} all-to-all(f32[8,4,256]{2,1,0:T(4,128)S(1)} %broadcast_in_dim.12), channel_id=1, replica_groups=mesh['kvp'=64,'tp'=8] {'tp'}, dimensions={0} | all-to-all | bytes 65536 | tf_op jit(solution)/shard_map/all_to_all | solution.py:21
  52.8 0.0 copy-done
  52.8 0.0 copy-done.2
  52.8 0.0 copy-done.3
  52.8 0.6 shard_map.106
  53.4 8.7 %all_to_all.33 = bf16[8,32,128]{2,1,0:T(8,128)(2,1)S(1)} all-to-all(bf16[8,32,128]{2,1,0:T(8,128)(2,1)S(1)} %convert_element_type.36), channel_id=1, replica_groups={{0,8,16,24,32,40,48,56},{64,72,80,88,96,104,112,120},{128,136,144,152,1..., dimensions={0} | all-to-all | bytes 131072 | tf_op jit(solution)/shard_map/all_to_all | solution.py:21
  62.2 14.5 %all_to_all.34 = bf16[8,32,128]{2,1,0:T(8,128)(2,1)S(1)} all-to-all(bf16[8,32,128]{2,1,0:T(8,128)(2,1)S(1)} %broadcast_in_dim.13), channel_id=1, replica_groups={{0,64,128,192,288,352,416,480},{8,72,136,200,296,360,424,488},{16,80,14..., dimensions={0} | all-to-all | bytes 131072 | tf_op jit(solution)/shard_map/all_to_all | solution.py:21
  76.7 9.1 %all_to_all.35.blocks_ref = bf16[8,13,128]{2,1,0:T(8,128)(2,1)S(1)} all-to-all(bf16[8,13,128]{2,1,0:T(8,128)(2,1)S(1)} %broadcast_in_dim.14), channel_id=1, replica_groups={{0,8,16,24,32,40,48,56},{64,72,80,88,96,104,112,120},{128,136,144,152,1..., dimensions={0} | all-to-all | bytes 53248 | tf_op jit(solution)/shard_map/all_to_all | solution.py:21
  85.8 0.7 shard_map.107
  (23 shorter events, 0.3 us)
Async XLA Ops:
  0.6 43.0 %copy-start.1 = (bf16[2048,256]{1,0:T(8,128)(2,1)S(1)}, bf16[2048,256]{1,0:T(8,128)(2,1)}, u32[]{:S(2)}) copy-start(bf16[2048,256]{1,0:T(8,128)(2,1)} %weight_ref.1) | copy-start | bytes 3145732
  2.4 50.4 %copy-start = (bf16[256,3328]{1,0:T(8,128)(2,1)S(1)}, bf16[256,3328]{1,0:T(8,128)(2,1)}, u32[]{:S(2)}) copy-start(bf16[256,3328]{1,0:T(8,128)(2,1)} %gate_ref.1) | copy-start | bytes 5111812
  2.4 50.3 %copy-start.2 = (bf16[4,256]{1,0:T(4,128)(2,1)S(1)}, bf16[4,256]{1,0:T(4,128)(2,1)}, u32[]{:S(2)}) copy-start(bf16[4,256]{1,0:T(4,128)(2,1)} %residual_ref.1) | copy-start | bytes 6148
  2.4 50.3 %copy-start.3 = (f32[256]{0:T(256)S(1)}, f32[256]{0:T(256)}, u32[]{:S(2)}) copy-start(f32[256]{0:T(256)} %param.15) | copy-start | bytes 3076

commit v4 on v3

--- a/solution.py
+++ b/solution.py
@@ -7,14 +7,19 @@
 
 NEAR = 8
 LANES = 128
+NEAR_LEAD = 6
+
+
+def led(group, by):
+    return group[by:] + group[:by]
 
 
 def teams(count):
     near = []
     for first in range(0, count, NEAR):
         turn = NEAR // 2 if 2 * first >= count else 0
-        near.append([first + (at ^ turn) for at in range(NEAR)])
-    return near, [list(far) for far in zip(*near)]
+        near.append(led([first + (at ^ turn) for at in range(NEAR)], NEAR_LEAD))
+    return near, [led(list(far), len(far) // 2) for far in zip(*near)]
 
 
 def exchange(blocks, axis, groups=None):
@@ -185,6 +190,7 @@
 ):
     rows, heads, head_dim = query.shape
     near, far = teams(lax.axis_size("kvp"))
+    tp = lax.axis_size("tp")
     vmem, hbm = pl.BlockSpec(memory_space=pltpu.VMEM), pl.BlockSpec(memory_space=pltpu.HBM)
     params = pltpu.CompilerParams(vmem_limit_bytes=16 * 2**20)
     sources = (lengths, query, key_cache, value_cache, up_weight)
@@ -231,7 +237,7 @@
         in_specs=[vmem] * 5,
         out_specs=(vmem,) * 2,
         compiler_params=params,
-    )(spread(projected, "tp"), residual, norm_gain.reshape(1, -1), gate_weight, up_weight)
+    )(spread(projected, "tp", [led(list(range(tp)), (tp // 2 + 1) % tp)]), residual, norm_gain.reshape(1, -1), gate_weight, up_weight)
 
     terms = exchange(terms.astype(jnp.bfloat16), "kvp", near)
     terms = jnp.sum(terms.astype(jnp.float32), axis=0)

time: 86.9 us -> 78.7 us (0.906)
  the two profiles are of different devices: /device:TPU:2 before, /device:TPU:4 now
where the time goes in v4:
time: 78.7 us; the launch traced here: 78.4 us
  blocking collectives  73.7 us (94%)
  Pallas kernels  3.51 us (4%)
  between operations  0.81 us (1%)
    all_to_all x6, blocking collectives, exchange(): lax.all_to_all(blocks, axis, 0, 0, axis_index_groups=groups, tiled=True)  73.7 us
    pallas_call x1, Pallas kernels, local(): pl.pallas_call(attend, out_shape=(pltpu.VMEM((rows, heads, head_dim), jnp...  1.76 us

profile of v4, /device:TPU:4, one launch (start us, length us, event | category | flops | bytes accessed | tf_op | source)
XLA Modules:
  0.0 78.4 jit_solution(971090325666942638)
XLA Ops:
  0.6 0.0 copy-start.1
  0.6 1.8 %shard_map.104 = (bf16[4,16,128]{2,1,0:T(8,128)(2,1)S(1)}, f32[8,128]{1,0:T(8,128)S(1)}, bf16[256,3328]{1,0:T(8,128)(2,1)S(1)}) custom-call(s32[4]{0:T(128)} %lengths_hbm.1, bf16[4,16,128]{2,1,0:T(8,128)(2,1)} %query_hbm.1, bf16[4,1,256,128]{3,2,1,0:T(8,128)(2,1)} %key_hbm.1, bf16[4,1,256,128]{3,2,1,0:T(8,128)(2,1)} %value_hbm.1, bf16[256,3328]{1,0:T(8,128)(2,1)} %others_0_.1), custom_call_target="tpu_custom_call" | custom-call | tf_op jit(solution)/shard_map/pallas_call | solution.py:197
  2.4 0.0 copy-start
  2.4 0.0 copy-start.2
  2.4 0.0 copy-start.3
  2.5 10.2 %all_to_all.30 = bf16[8,72,128]{2,1,0:T(8,128)(2,1)S(1)} all-to-all(bf16[8,72,128]{2,1,0:T(8,128)(2,1)S(1)} %broadcast_in_dim.10), channel_id=1, replica_groups={{48,56,0,8,16,24,32,40},{112,120,64,72,80,88,96,104},{176,184,128,136,1..., dimensions={0} | all-to-all | bytes 294912 | tf_op jit(solution)/shard_map/all_to_all | solution.py:26
  12.8 0.1 multiply_reduce_fusion
  12.9 23.4 %all_to_all.31.blocks_ref = bf16[8,72,128]{2,1,0:T(8,128)(2,1)S(1)} all-to-all(bf16[8,72,128]{2,1,0:T(8,128)(2,1)S(1)} %broadcast_in_dim.11), channel_id=1, replica_groups={{272,336,400,464,48,112,176,240},{280,344,408,472,56,120,184,248},{288,..., dimensions={0} | all-to-all | bytes 294912 | tf_op jit(solution)/shard_map/all_to_all | solution.py:26
  36.3 0.0 copy-done.1
  36.3 0.5 shard_map.105
  36.8 7.4 %all_to_all.32.terms_ref = f32[8,4,256]{2,1,0:T(4,128)S(1)} all-to-all(f32[8,4,256]{2,1,0:T(4,128)S(1)} %broadcast_in_dim.12), channel_id=1, replica_groups={{5,6,7,0,1,2,3,4},{13,14,15,8,9,10,11,12},{21,22,23,16,17,18,19,20},{29..., dimensions={0} | all-to-all | bytes 65536 | tf_op jit(solution)/shard_map/all_to_all | solution.py:26
  44.3 0.0 copy-done
  44.3 0.0 copy-done.2
  44.3 0.0 copy-done.3
  44.3 0.6 shard_map.106
  44.9 8.4 %all_to_all.33 = bf16[8,32,128]{2,1,0:T(8,128)(2,1)S(1)} all-to-all(bf16[8,32,128]{2,1,0:T(8,128)(2,1)S(1)} %convert_element_type.36), channel_id=1, replica_groups={{48,56,0,8,16,24,32,40},{112,120,64,72,80,88,96,104},{176,184,128,136,1..., dimensions={0} | all-to-all | bytes 131072 | tf_op jit(solution)/shard_map/all_to_all | solution.py:26
  53.3 16.0 %all_to_all.34 = bf16[8,32,128]{2,1,0:T(8,128)(2,1)S(1)} all-to-all(bf16[8,32,128]{2,1,0:T(8,128)(2,1)S(1)} %broadcast_in_dim.13), channel_id=1, replica_groups={{272,336,400,464,48,112,176,240},{280,344,408,472,56,120,184,248},{288,..., dimensions={0} | all-to-all | bytes 131072 | tf_op jit(solution)/shard_map/all_to_all | solution.py:26
  69.4 8.3 %all_to_all.35.blocks_ref = bf16[8,13,128]{2,1,0:T(8,128)(2,1)S(1)} all-to-all(bf16[8,13,128]{2,1,0:T(8,128)(2,1)S(1)} %broadcast_in_dim.14), channel_id=1, replica_groups={{48,56,0,8,16,24,32,40},{112,120,64,72,80,88,96,104},{176,184,128,136,1..., dimensions={0} | all-to-all | bytes 53248 | tf_op jit(solution)/shard_map/all_to_all | solution.py:26
  77.7 0.7 shard_map.107
  (23 shorter events, 0.3 us)
Async XLA Ops:
  0.6 35.7 %copy-start.1 = (bf16[2048,256]{1,0:T(8,128)(2,1)S(1)}, bf16[2048,256]{1,0:T(8,128)(2,1)}, u32[]{:S(2)}) copy-start(bf16[2048,256]{1,0:T(8,128)(2,1)} %weight_ref.1) | copy-start | bytes 3145732
  2.4 41.9 %copy-start = (bf16[256,3328]{1,0:T(8,128)(2,1)S(1)}, bf16[256,3328]{1,0:T(8,128)(2,1)}, u32[]{:S(2)}) copy-start(bf16[256,3328]{1,0:T(8,128)(2,1)} %gate_ref.1) | copy-start | bytes 5111812
  2.4 41.8 %copy-start.2 = (bf16[4,256]{1,0:T(4,128)(2,1)S(1)}, bf16[4,256]{1,0:T(4,128)(2,1)}, u32[]{:S(2)}) copy-start(bf16[4,256]{1,0:T(4,128)(2,1)} %residual_ref.1) | copy-start | bytes 6148
  2.4 41.8 %copy-start.3 = (f32[256]{0:T(256)S(1)}, f32[256]{0:T(256)}, u32[]{:S(2)}) copy-start(f32[256]{0:T(256)} %param.15) | copy-start | bytes 3076

commit v5 on v4

--- a/solution.py
+++ b/solution.py
@@ -7,6 +7,7 @@
 
 NEAR = 8
 LANES = 128
+TURN = NEAR // 2
 NEAR_LEAD = 6
 
 
@@ -19,7 +20,7 @@
     for first in range(0, count, NEAR):
         turn = NEAR // 2 if 2 * first >= count else 0
         near.append(led([first + (at ^ turn) for at in range(NEAR)], NEAR_LEAD))
-    return near, [led(list(far), len(far) // 2) for far in zip(*near)]
+    return near, [led(list(far), count // NEAR // 2) for far in zip(*near)]
 
 
 def exchange(blocks, axis, groups=None):
@@ -173,7 +174,8 @@
     rows = stream_ref.shape[0]
     halves = NEAR // rows
     deep = blocks_ref.shape[1]
-    wide_ref[...] = blocks_ref[...].astype(jnp.float32)
+    wide_ref[:TURN] = blocks_ref[TURN:].astype(jnp.float32)
+    wide_ref[TURN:] = blocks_ref[:TURN].astype(jnp.float32)
     for half in range(halves):
         for at in range(deep):
             piece = wide_ref[pl.ds(half, rows, stride=halves), at, :]
@@ -214,7 +216,7 @@
     )(*[pltpu.with_memory_space_constraint(source, pltpu.HBM) for source in sources])
     out = out.reshape(rows * heads, head_dim)
     out, peak, total = combine(spread(pack(out, stats), "kvp", near))
-    blocks = spread(pack(out, stacked(peak, total)), "kvp", far)
+    blocks = spread(pack(out, stacked(peak, total)), "kvp", [led(team, 1) for team in far])
     block_width = out_weight.shape[1]
     projected = pl.pallas_call(
         project,
@@ -239,7 +241,7 @@
         compiler_params=params,
     )(spread(projected, "tp", [led(list(range(tp)), (tp // 2 + 1) % tp)]), residual, norm_gain.reshape(1, -1), gate_weight, up_weight)
 
-    terms = exchange(terms.astype(jnp.bfloat16), "kvp", near)
+    terms = exchange(terms.astype(jnp.bfloat16), "kvp", [led(team, TURN) for team in near])
     terms = jnp.sum(terms.astype(jnp.float32), axis=0)
     pair = jnp.stack(split_pair(terms[2 * deep] + terms[2 * deep + 1]))
     terms = jnp.concatenate([terms[: 2 * deep], pair, terms[2 * deep + 2 :]]).astype(jnp.bfloat16)

time: 78.7 us -> 78.2 us (level)
  no operation moved by 1% of the time
where the time goes in v5:
time: 78.2 us; the launch traced here: 77.9 us
  blocking collectives  73.2 us (94%)
  Pallas kernels  3.51 us (4%)
  between operations  0.81 us (1%)
    all_to_all x6, blocking collectives, exchange(): lax.all_to_all(blocks, axis, 0, 0, axis_index_groups=groups, tiled=True)  73.2 us
    pallas_call x1, Pallas kernels, local(): pl.pallas_call(attend, out_shape=(pltpu.VMEM((rows, heads, head_dim), jnp...  1.76 us

profile of v5, /device:TPU:4, one launch (start us, length us, event | category | flops | bytes accessed | tf_op | source)
XLA Modules:
  0.0 77.9 jit_solution(17576430966072205368)
XLA Ops:
  0.6 0.0 copy-start.1
  0.6 1.8 %shard_map.104 = (bf16[4,16,128]{2,1,0:T(8,128)(2,1)S(1)}, f32[8,128]{1,0:T(8,128)S(1)}, bf16[256,3328]{1,0:T(8,128)(2,1)S(1)}) custom-call(s32[4]{0:T(128)} %lengths_hbm.1, bf16[4,16,128]{2,1,0:T(8,128)(2,1)} %query_hbm.1, bf16[4,1,256,128]{3,2,1,0:T(8,128)(2,1)} %key_hbm.1, bf16[4,1,256,128]{3,2,1,0:T(8,128)(2,1)} %value_hbm.1, bf16[256,3328]{1,0:T(8,128)(2,1)} %others_0_.1), custom_call_target="tpu_custom_call" | custom-call | tf_op jit(solution)/shard_map/pallas_call | solution.py:199
  2.4 0.0 copy-start
  2.4 0.0 copy-start.2
  2.4 0.0 copy-start.3
  2.5 10.2 %all_to_all.30 = bf16[8,72,128]{2,1,0:T(8,128)(2,1)S(1)} all-to-all(bf16[8,72,128]{2,1,0:T(8,128)(2,1)S(1)} %broadcast_in_dim.10), channel_id=1, replica_groups={{48,56,0,8,16,24,32,40},{112,120,64,72,80,88,96,104},{176,184,128,136,1..., dimensions={0} | all-to-all | bytes 294912 | tf_op jit(solution)/shard_map/all_to_all | solution.py:27
  12.8 0.1 multiply_reduce_fusion
  12.9 23.8 %all_to_all.31.blocks_ref = bf16[8,72,128]{2,1,0:T(8,128)(2,1)S(1)} all-to-all(bf16[8,72,128]{2,1,0:T(8,128)(2,1)S(1)} %broadcast_in_dim.11), channel_id=1, replica_groups={{336,400,464,48,112,176,240,272},{344,408,472,56,120,184,248,280},{352,..., dimensions={0} | all-to-all | bytes 294912 | tf_op jit(solution)/shard_map/all_to_all | solution.py:27
  36.8 0.0 copy-done.1
  36.8 0.5 shard_map.105
  37.3 7.4 %all_to_all.32.terms_ref = f32[8,4,256]{2,1,0:T(4,128)S(1)} all-to-all(f32[8,4,256]{2,1,0:T(4,128)S(1)} %broadcast_in_dim.12), channel_id=1, replica_groups={{5,6,7,0,1,2,3,4},{13,14,15,8,9,10,11,12},{21,22,23,16,17,18,19,20},{29..., dimensions={0} | all-to-all | bytes 65536 | tf_op jit(solution)/shard_map/all_to_all | solution.py:27
  44.7 0.0 copy-done
  44.7 0.0 copy-done.2
  44.7 0.0 copy-done.3
  44.7 0.6 shard_map.106
  45.3 8.3 %all_to_all.33 = bf16[8,32,128]{2,1,0:T(8,128)(2,1)S(1)} all-to-all(bf16[8,32,128]{2,1,0:T(8,128)(2,1)S(1)} %convert_element_type.36), channel_id=1, replica_groups={{16,24,32,40,48,56,0,8},{80,88,96,104,112,120,64,72},{144,152,160,168,1..., dimensions={0} | all-to-all | bytes 131072 | tf_op jit(solution)/shard_map/all_to_all | solution.py:27
  53.7 15.1 %all_to_all.34 = bf16[8,32,128]{2,1,0:T(8,128)(2,1)S(1)} all-to-all(bf16[8,32,128]{2,1,0:T(8,128)(2,1)S(1)} %broadcast_in_dim.13), channel_id=1, replica_groups={{272,336,400,464,48,112,176,240},{280,344,408,472,56,120,184,248},{288,..., dimensions={0} | all-to-all | bytes 131072 | tf_op jit(solution)/shard_map/all_to_all | solution.py:27
  68.8 8.4 %all_to_all.35.blocks_ref = bf16[8,13,128]{2,1,0:T(8,128)(2,1)S(1)} all-to-all(bf16[8,13,128]{2,1,0:T(8,128)(2,1)S(1)} %broadcast_in_dim.14), channel_id=1, replica_groups={{48,56,0,8,16,24,32,40},{112,120,64,72,80,88,96,104},{176,184,128,136,1..., dimensions={0} | all-to-all | bytes 53248 | tf_op jit(solution)/shard_map/all_to_all | solution.py:27
  77.2 0.7 shard_map.107
  (23 shorter events, 0.3 us)
Async XLA Ops:
  0.6 36.1 %copy-start.1 = (bf16[2048,256]{1,0:T(8,128)(2,1)S(1)}, bf16[2048,256]{1,0:T(8,128)(2,1)}, u32[]{:S(2)}) copy-start(bf16[2048,256]{1,0:T(8,128)(2,1)} %weight_ref.1) | copy-start | bytes 3145732
  2.4 42.3 %copy-start = (bf16[256,3328]{1,0:T(8,128)(2,1)S(1)}, bf16[256,3328]{1,0:T(8,128)(2,1)}, u32[]{:S(2)}) copy-start(bf16[256,3328]{1,0:T(8,128)(2,1)} %gate_ref.1) | copy-start | bytes 5111812
  2.4 42.3 %copy-start.2 = (bf16[4,256]{1,0:T(4,128)(2,1)S(1)}, bf16[4,256]{1,0:T(4,128)(2,1)}, u32[]{:S(2)}) copy-start(bf16[4,256]{1,0:T(4,128)(2,1)} %residual_ref.1) | copy-start | bytes 6148
  2.4 42.3 %copy-start.3 = (f32[256]{0:T(256)S(1)}, f32[256]{0:T(256)}, u32[]{:S(2)}) copy-start(f32[256]{0:T(256)} %param.15) | copy-start | bytes 3076

commit v6 on v5

--- a/solution.py
+++ b/solution.py
@@ -215,7 +215,7 @@
         compiler_params=params,
     )(*[pltpu.with_memory_space_constraint(source, pltpu.HBM) for source in sources])
     out = out.reshape(rows * heads, head_dim)
-    out, peak, total = combine(spread(pack(out, stats), "kvp", near))
+    out, peak, total = combine(spread(pack(out, stats), "kvp", [led(team, TURN) for team in near]))
     blocks = spread(pack(out, stacked(peak, total)), "kvp", [led(team, 1) for team in far])
     block_width = out_weight.shape[1]
     projected = pl.pallas_call(

time: 78.2 us -> 78 us (level)
  no operation moved by 1% of the time
where the time goes in v6:
time: 78 us; the launch traced here: 77.7 us
  blocking collectives  73 us (94%)
  Pallas kernels  3.51 us (4%)
  between operations  0.81 us (1%)
    all_to_all x6, blocking collectives, exchange(): lax.all_to_all(blocks, axis, 0, 0, axis_index_groups=groups, tiled=True)  73 us
    pallas_call x1, Pallas kernels, local(): pl.pallas_call(attend, out_shape=(pltpu.VMEM((rows, heads, head_dim), jnp...  1.76 us

profile of v6, /device:TPU:4, one launch (start us, length us, event | category | flops | bytes accessed | tf_op | source)
XLA Modules:
  0.0 77.7 jit_solution(2437016786691365106)
XLA Ops:
  0.6 0.0 copy-start.1
  0.6 1.8 %shard_map.104 = (bf16[4,16,128]{2,1,0:T(8,128)(2,1)S(1)}, f32[8,128]{1,0:T(8,128)S(1)}, bf16[256,3328]{1,0:T(8,128)(2,1)S(1)}) custom-call(s32[4]{0:T(128)} %lengths_hbm.1, bf16[4,16,128]{2,1,0:T(8,128)(2,1)} %query_hbm.1, bf16[4,1,256,128]{3,2,1,0:T(8,128)(2,1)} %key_hbm.1, bf16[4,1,256,128]{3,2,1,0:T(8,128)(2,1)} %value_hbm.1, bf16[256,3328]{1,0:T(8,128)(2,1)} %others_0_.1), custom_call_target="tpu_custom_call" | custom-call | tf_op jit(solution)/shard_map/pallas_call | solution.py:199
  2.4 0.0 copy-start
  2.4 0.0 copy-start.2
  2.4 0.0 copy-start.3
  2.5 11.0 %all_to_all.30 = bf16[8,72,128]{2,1,0:T(8,128)(2,1)S(1)} all-to-all(bf16[8,72,128]{2,1,0:T(8,128)(2,1)S(1)} %broadcast_in_dim.10), channel_id=1, replica_groups={{16,24,32,40,48,56,0,8},{80,88,96,104,112,120,64,72},{144,152,160,168,1..., dimensions={0} | all-to-all | bytes 294912 | tf_op jit(solution)/shard_map/all_to_all | solution.py:27
  13.6 0.1 multiply_reduce_fusion
  13.8 22.6 %all_to_all.31.blocks_ref = bf16[8,72,128]{2,1,0:T(8,128)(2,1)S(1)} all-to-all(bf16[8,72,128]{2,1,0:T(8,128)(2,1)S(1)} %broadcast_in_dim.11), channel_id=1, replica_groups={{336,400,464,48,112,176,240,272},{344,408,472,56,120,184,248,280},{352,..., dimensions={0} | all-to-all | bytes 294912 | tf_op jit(solution)/shard_map/all_to_all | solution.py:27
  36.4 0.0 copy-done.1
  36.4 0.5 shard_map.105
  36.9 7.4 %all_to_all.32.terms_ref = f32[8,4,256]{2,1,0:T(4,128)S(1)} all-to-all(f32[8,4,256]{2,1,0:T(4,128)S(1)} %broadcast_in_dim.12), channel_id=1, replica_groups={{5,6,7,0,1,2,3,4},{13,14,15,8,9,10,11,12},{21,22,23,16,17,18,19,20},{29..., dimensions={0} | all-to-all | bytes 65536 | tf_op jit(solution)/shard_map/all_to_all | solution.py:27
  44.4 0.0 copy-done
  44.4 0.0 copy-done.2
  44.4 0.0 copy-done.3
  44.4 0.6 shard_map.106
  45.0 8.5 %all_to_all.33 = bf16[8,32,128]{2,1,0:T(8,128)(2,1)S(1)} all-to-all(bf16[8,32,128]{2,1,0:T(8,128)(2,1)S(1)} %convert_element_type.36), channel_id=1, replica_groups={{16,24,32,40,48,56,0,8},{80,88,96,104,112,120,64,72},{144,152,160,168,1..., dimensions={0} | all-to-all | bytes 131072 | tf_op jit(solution)/shard_map/all_to_all | solution.py:27
  53.5 15.1 %all_to_all.34 = bf16[8,32,128]{2,1,0:T(8,128)(2,1)S(1)} all-to-all(bf16[8,32,128]{2,1,0:T(8,128)(2,1)S(1)} %broadcast_in_dim.13), channel_id=1, replica_groups={{272,336,400,464,48,112,176,240},{280,344,408,472,56,120,184,248},{288,..., dimensions={0} | all-to-all | bytes 131072 | tf_op jit(solution)/shard_map/all_to_all | solution.py:27
  68.6 8.4 %all_to_all.35.blocks_ref = bf16[8,13,128]{2,1,0:T(8,128)(2,1)S(1)} all-to-all(bf16[8,13,128]{2,1,0:T(8,128)(2,1)S(1)} %broadcast_in_dim.14), channel_id=1, replica_groups={{48,56,0,8,16,24,32,40},{112,120,64,72,80,88,96,104},{176,184,128,136,1..., dimensions={0} | all-to-all | bytes 53248 | tf_op jit(solution)/shard_map/all_to_all | solution.py:27
  77.0 0.7 shard_map.107
  (23 shorter events, 0.3 us)
Async XLA Ops:
  0.6 35.8 %copy-start.1 = (bf16[2048,256]{1,0:T(8,128)(2,1)S(1)}, bf16[2048,256]{1,0:T(8,128)(2,1)}, u32[]{:S(2)}) copy-start(bf16[2048,256]{1,0:T(8,128)(2,1)} %weight_ref.1) | copy-start | bytes 3145732
  2.4 41.9 %copy-start = (bf16[256,3328]{1,0:T(8,128)(2,1)S(1)}, bf16[256,3328]{1,0:T(8,128)(2,1)}, u32[]{:S(2)}) copy-start(bf16[256,3328]{1,0:T(8,128)(2,1)} %gate_ref.1) | copy-start | bytes 5111812
  2.4 41.9 %copy-start.2 = (bf16[4,256]{1,0:T(4,128)(2,1)S(1)}, bf16[4,256]{1,0:T(4,128)(2,1)}, u32[]{:S(2)}) copy-start(bf16[4,256]{1,0:T(4,128)(2,1)} %residual_ref.1) | copy-start | bytes 6148
  2.4 41.9 %copy-start.3 = (f32[256]{0:T(256)S(1)}, f32[256]{0:T(256)}, u32[]{:S(2)}) copy-start(f32[256]{0:T(256)} %param.15) | copy-start | bytes 3076
